TPU v7x, 32 devices: a whole 2x2x4 slice. The times are simulated.
32 devices in a mesh: dp: 8 (over z, core), pack: 4 (over y, x).
Axes of the slice: x: 2, y: 2, z: 4, core: 2. Of those that a mesh axis runs over, the one named last changes fastest.
Arguments:
- images: bfloat16 [64, 1152], P(('dp', 'pack')), may hold values from -6 to 6
- captions: bfloat16 [128, 1152], P(('dp', 'pack')), may hold values from -6 to 6
- caption_owner: int32 [128], P(('dp', 'pack')), may hold values from 0 to 7, as said below
- caption_count: int32 [32], P(('dp', 'pack')), may hold values from 0 to 4, as said below
- log_scale: float32 [1], replicated, may hold values from 1.6 to 2.6
- bias: float32 [1], replicated, may hold values from -3 to 0
Outputs:
- row_loss: float32 [64], P(('dp', 'pack'))
- grad_images: float32 [64, 1152], P(('dp', 'pack'))
- grad_captions: float32 [128, 1152], P(('dp', 'pack'))
Inputs may be any that keep to these rules, and one draw needn't show every extreme that they name: `caption_owner`: within each pair block, the filled slots of its 4 devices name every one of its 8 pairs exactly once; values in empty slots are arbitrary. `caption_count`: the counts of one pair block's devices sum to 8.
All inputs are finite; a program needn't handle non-finite values.
Results may differ from a plain program's by a relative error of at most 0.0043.
Values may be sent and summed in bfloat16 or wider, within the bound.
No kernel may reach another device: no remote copies, remote signals or barrier semaphores. Data moves between devices by JAX's collectives and lax.ppermute only.
A program may use at most 64 MiB of HBM per device.

v0:
```python
import jax
import jax.numpy as jnp
from jax import lax
from jax.sharding import PartitionSpec as P

eps = 1e-06


def normalize(block_rows):
    floats = block_rows.astype(jnp.float32)
    inverse = lax.rsqrt(jnp.sum(floats * floats, axis=-1, keepdims=True) + eps)
    return (floats * inverse, inverse)


def unnormalize(unit_rows, inverse, upstream):
    return inverse * (upstream - unit_rows * jnp.sum(unit_rows * upstream, axis=-1, keepdims=True))


def body(images, captions, caption_owner, caption_count, log_scale, bias):
    pair_rows = images.shape[0]
    packers = lax.axis_size("pack")
    cycle_blocks = lax.axis_size("dp")
    group_rows = pair_rows * packers
    all_pairs = group_rows * cycle_blocks
    slot_count = captions.shape[0]
    cycle_index = lax.axis_index("dp")
    pack_index = lax.axis_index("pack")
    filled = jnp.arange(slot_count, dtype=jnp.int32) < caption_count[0]
    routing = jnp.logical_and(
        caption_owner[:, None] == jnp.arange(group_rows, dtype=jnp.int32)[None, :], filled[:, None]
    )
    outgoing = lax.dot_general(
        routing.astype(jnp.bfloat16),
        captions,
        (((0,), (0,)), ((), ())),
        preferred_element_type=jnp.float32,
    ).astype(jnp.bfloat16)
    incoming = lax.all_to_all(
        outgoing.reshape(packers, pair_rows, outgoing.shape[1]),
        "pack",
        split_axis=0,
        concat_axis=0,
        tiled=True,
    )
    owned_texts = jnp.sum(incoming.astype(jnp.float32), axis=0)
    text_unit, text_inv = normalize(owned_texts.astype(jnp.bfloat16))
    text16 = text_unit.astype(jnp.bfloat16)
    image_unit, image_inv = normalize(images)
    image16 = image_unit.astype(jnp.bfloat16)
    image_rows = lax.all_gather(image16, "pack", axis=0, tiled=True)
    logit_scale = jnp.exp(log_scale[0])
    logit_shift = bias[0]
    image_ids = cycle_index * group_rows + jnp.arange(group_rows, dtype=jnp.int32)
    column_texts = lax.all_gather(text16, "dp", axis=0, tiled=True)
    positions = jnp.arange(column_texts.shape[0], dtype=jnp.int32)
    text_ids = positions // pair_rows * group_rows + pack_index * pair_rows + positions % pair_rows
    logits = (
        logit_scale
        * lax.dot_general(
            image_rows, column_texts, (((1,), (1,)), ((), ())), preferred_element_type=jnp.float32
        )
        + logit_shift
    )
    labels = jnp.where(image_ids[:, None] == text_ids[None, :], 1.0, -1.0).astype(jnp.float32)
    losses = jnp.sum(jax.nn.softplus(-labels * logits), axis=1)
    score_weights = (-labels * jax.nn.sigmoid(-labels * logits)).astype(jnp.bfloat16)
    grad_sum = jnp.dot(score_weights, column_texts, preferred_element_type=jnp.float32)
    row_loss, grad_unit = (
        lax.psum_scatter(losses / all_pairs, "pack", scatter_dimension=0, tiled=True),
        lax.psum_scatter(logit_scale * grad_sum, "pack", scatter_dimension=0, tiled=True),
    )
    grad_images = unnormalize(image_unit, image_inv, grad_unit)
    text_grad = lax.psum_scatter(
        logit_scale
        * lax.dot_general(
            score_weights, image_rows, (((0,), (0,)), ((), ())), preferred_element_type=jnp.float32
        ),
        "dp",
        scatter_dimension=0,
        tiled=True,
    )
    owner_grad = unnormalize(text_unit, text_inv, text_grad)
    returned = lax.all_gather(owner_grad, "pack", axis=0, tiled=True)
    picked = jnp.dot(routing.astype(jnp.float32), returned, precision=lax.Precision.HIGHEST)
    return (row_loss, grad_images, picked)


def solution(mesh):
    placed = (
        P(("dp", "pack"), None),
        P(("dp", "pack"), None),
        P(("dp", "pack")),
        P(("dp", "pack")),
        P(),
        P(),
    )
    return jax.shard_map(
        body,
        mesh=mesh,
        in_specs=placed,
        out_specs=(P(("dp", "pack")), P(("dp", "pack"), None), P(("dp", "pack"), None)),
        check_vma=False,
    )
```

profile of v0, /device:TPU:0, one launch (start us, length us, event | category | flops | bytes accessed | tf_op | source)
XLA Modules:
  0.0 111.9 jit_solution(8705925612514551141)
XLA Ops:
  7.2 0.0 copy-start
  7.8 0.0 copy-start.2
  7.9 0.0 copy-done
  7.9 0.6 copy-done.2
  8.5 0.3 convolution_convert_fusion
  8.8 0.6 reshape.56
  9.4 5.2 %all-to-all-start = ((bf16[4,2,1152]{2,1,0:T(2,128)(2,1)}), bf16[4,2,1152]{2,1,0:T(2,128)(2,1)S(1)}, u32[]{:S(2)}, u32[]{:S(2)}) async-start(bf16[4,2,1152]{2,1,0:T(2,128)(2,1)} %reshape.56), calls=%async_computation | async-start | bytes 36864 | tf_op jit(solution)/shard_map/all_to_all | solution.py:38
  14.5 0.0 all-reduce.6.cloned.1.call-start
  14.5 0.0 copy-start.1
  14.6 0.7 copy-done.1
  15.2 0.1 fusion.15
  15.4 0.1 fusion.18
  16.8 0.0 copy-start.4
  16.8 0.6 copy-done.4
  17.5 0.0 copy-start.3
  17.5 0.6 dynamic-slice.4
  18.0 0.1 copy-done.3
  18.1 0.7 dynamic-slice
  20.0 8.7 %all-gather = bf16[4,2,1152]{2,1,0:T(2,128)(2,1)S(1)} all-gather(bf16[1,2,1152]{2,1,0:T(2,128)(2,1)S(1)} %fusion.18), channel_id=1, replica_groups=mesh['dp'=8,'pack'=4] {'pack'}, dimensions={0}, use_global_device_ids=true | all-gather | bytes 23040 | tf_op jit(solution)/shard_map/all_gather | solution.py:50
  28.7 0.0 all-to-all-done
  28.8 0.1 fusion.16
  28.9 0.1 fusion.17
  29.0 14.2 %all-gather.1 = bf16[8,2,1152]{2,1,0:T(2,128)(2,1)S(1)} all-gather(bf16[1,2,1152]{2,1,0:T(2,128)(2,1)S(1)} %fusion.17), channel_id=1, replica_groups=mesh['dp'=8,'pack'=4] {'dp'}, dimensions={0}, use_global_device_ids=true | all-gather | bytes 41472 | tf_op jit(solution)/shard_map/all_gather | solution.py:54
  43.2 0.2 fusion.19
  43.5 0.2 convolution_multiply_fusion.1
  43.7 0.9 convolution_multiply_fusion
  44.6 0.0 all-reduce.6.cloned.1.call-update
  44.6 15.8 %all-reduce.3 = (f32[8]{0:T(128)S(1)}, f32[8,1152]{1,0:T(8,128)S(1)}) all-reduce(f32[8]{0:T(128)S(1)} %broadcast_multiply_fusion, f32[8,1152]{1,0:T(8,128)S(1)} %convolution_multiply_fusion.1), channel_id=2, replica_groups=mesh['dp'=8,'pack'=4] {'pack'}, use_global_device_ids=true, to_apply=%region_4.5.clone | all-reduce | flops 9224 | bytes 73792
  60.4 0.2 fusion.12
  60.6 0.7 fusion.14
  61.3 0.6 dynamic-slice.1
  61.8 32.4 %all-reduce.6.cloned.1.call-done = f32[16,1152]{1,0:T(8,128)} async-done(((f32[16,1152]{1,0:T(8,128)}), f32[16,1152]{1,0:T(8,128)}) %all-reduce.6.cloned.1.call-update) | async-done | bytes 73744
  94.3 1.0 fusion.8
  95.2 0.8 fusion.11
  96.1 8.2 %all-gather.2 = f32[4,2,1152]{2,1,0:T(2,128)S(1)} all-gather(f32[1,2,1152]{2,1,0:T(2,128)S(1)} %fusion.11), channel_id=1, replica_groups=mesh['dp'=8,'pack'=4] {'pack'}, dimensions={0}, use_global_device_ids=true | all-gather | bytes 46080 | tf_op jit(solution)/shard_map/all_gather | solution.py:83
  104.3 0.8 fusion.21
  (10 shorter events, 0.1 us)
Async XLA Ops:
  7.2 0.7 copy-start
  7.8 0.7 copy-start.2
  9.4 19.3 %all-to-all-start = ((bf16[4,2,1152]{2,1,0:T(2,128)(2,1)}), bf16[4,2,1152]{2,1,0:T(2,128)(2,1)S(1)}, u32[]{:S(2)}, u32[]{:S(2)}) async-start(bf16[4,2,1152]{2,1,0:T(2,128)(2,1)} %reshape.56), calls=%async_computation | async-start | bytes 36864 | tf_op jit(solution)/shard_map/all_to_all | solution.py:38
  14.5 79.7 %all-reduce.6.cloned.1.call-start = ((), (), s32[]{:S(2)}) async-start(), calls=%async_computation.1 | async-start | bytes 147456
  14.5 0.7 copy-start.1
  16.8 0.7 copy-start.4
  17.5 0.7 copy-start.3
Sparse Core Ops, SparseCore 0:
  44.7 49.5 all-reduce.5
where the time goes:
time: 113 us; the launch traced here: 112 us
  blocking collectives  46.9 us (42%)
  waiting for transfers between devices  32.4 us (29%)
  between operations  17.4 us (15%)
  starting transfers between devices  5.17 us (5%)
  local copies, waits for them, and re-layouts  4.56 us (4%)
  other arithmetic  3.14 us (3%)
  matrix products  2.41 us (2%)
    unnamed x2, waiting for transfers between devices  32.4 us
    unnamed x1, blocking collectives  15.8 us
    all_gather x1, blocking collectives, body(): column_texts = lax.all_gather(text16, 'dp', axis=0, tiled=True)  14.2 us
    all_gather x1, blocking collectives, body(): image_rows = lax.all_gather(image16, 'pack', axis=0, tiled=True)  8.67 us
    all_gather x1, blocking collectives, body(): returned = lax.all_gather(owner_grad, 'pack', axis=0, tiled=True)  8.15 us
    all_to_all x1, starting transfers between devices, body(): lax.all_to_all(outgoing.reshape(packers, pair_rows, outgoing.shape[1]), '...  5.16 us
    unnamed x16, local copies, waits for them, and re-layouts  3.93 us
  transfers between devices with their start and end apart: 2, of which 1 were waited for; matrix products, arithmetic and copies ran while one was open for 3% of the time, Pallas kernels for 0%

commit v1 on v0

v1 whole, which is shorter than its diff:
```python
import functools

import jax
import jax.numpy as jnp
from jax import lax
from jax.experimental import pallas as pl
from jax.experimental.pallas import tpu as pltpu
from jax.sharding import Mesh
from jax.sharding import PartitionSpec as P

eps = 1e-06
ROWS = 8
CHUNK = 16


def unit_rows(rows):
    floats = rows.astype(jnp.float32)
    inverse = lax.rsqrt(jnp.sum(floats * floats, axis=-1, keepdims=True) + eps)
    return floats * inverse, inverse


def pack_kernel(images_ref, captions_ref, owner_ref, count_ref, sent_ref):
    slots, width = captions_ref.shape
    images, _ = unit_rows(images_ref[...])
    captions, _ = unit_rows(captions_ref[...])
    left = ROWS - images_ref.shape[0] - slots
    lanes = lax.broadcasted_iota(jnp.int32, (left, width), 1)
    codes = jnp.zeros((left, width), jnp.float32)
    for slot in range(slots):
        code = jnp.where(slot < count_ref[0], owner_ref[slot], -1).astype(jnp.float32)
        codes = jnp.where(lanes == slot, code, codes)
    block = jnp.concatenate([images, captions, codes], axis=0).astype(jnp.bfloat16)

    def put(receiver):
        sent_ref[pl.ds(receiver * ROWS, ROWS), :] = block

    receivers = sent_ref.shape[0] // ROWS
    if receivers <= 16:
        for receiver in range(receivers):
            put(receiver)
    else:
        pl.loop(0, receivers)(put)


def pair_kernel(
    chips,
    packers,
    where_ref,
    owner_ref,
    count_ref,
    scale_ref,
    bias_ref,
    images_ref,
    captions_ref,
    mine_ref,
    other_ref,
    loss_ref,
    grad_images_ref,
    grad_captions_ref,
):
    pair_rows = images_ref.shape[0]
    slots, width = captions_ref.shape
    group_rows = pair_rows * packers
    chip_me, core_me, pack_me = where_ref[0], where_ref[1], where_ref[2]
    cycle_me = chip_me * 2 + core_me
    me = cycle_me * packers + pack_me
    devices = chips * 2 * packers
    chunk_rows = CHUNK * ROWS
    logit_scale = jnp.exp(jnp.full((1, 1), scale_ref[0], jnp.float32))
    logit_shift = bias_ref[0]

    images, images_inv = unit_rows(images_ref[...])
    captions, captions_inv = unit_rows(captions_ref[...])
    filler = jnp.zeros((ROWS - pair_rows - slots, width), jnp.float32)
    own = jnp.concatenate([images, captions, filler], axis=0)
    own_inv = jnp.concatenate([images_inv, captions_inv, filler[:, :1]], axis=0)
    own16 = own.astype(jnp.bfloat16)

    own_at = lax.broadcasted_iota(jnp.int32, (ROWS, 1), 0)
    own_pair = jnp.where(own_at < pair_rows, me * pair_rows + own_at, -1)
    for slot in range(slots):
        pair = jnp.where(slot < count_ref[0], cycle_me * group_rows + owner_ref[slot], -1)
        own_pair = jnp.where(own_at == pair_rows + slot, pair, own_pair)
    own_is_image = own_at < pair_rows

    column = lax.broadcasted_iota(jnp.int32, (1, chunk_rows), 1)
    column_at = column % ROWS
    column_is_image = column_at < pair_rows
    column_is_slot = jnp.logical_and(column_at >= pair_rows, column_at < pair_rows + slots)
    spread = (
        lax.broadcasted_iota(jnp.int32, (128, chunk_rows), 0)
        == lax.broadcasted_iota(jnp.int32, (128, chunk_rows), 1) % ROWS - pair_rows
    ).astype(jnp.bfloat16)
    code_row = lax.broadcasted_iota(jnp.int32, (chunk_rows, chunk_rows), 0)
    code_column = lax.broadcasted_iota(jnp.int32, (chunk_rows, chunk_rows), 1)
    code_here = code_row == code_column // ROWS * ROWS + pair_rows + slots

    def one_chunk(rows_ref, core_from, chunk, totals):
        loss, upstream = totals
        rows = rows_ref[pl.ds(chunk * chunk_rows, chunk_rows), :]
        codes = jnp.dot(rows[:, :128], spread, preferred_element_type=jnp.float32)
        codes = jnp.sum(jnp.where(code_here, codes, 0.0), axis=0, keepdims=True).astype(jnp.int32)
        block = chunk * CHUNK + column // ROWS
        cycle_at = block // packers * 2 + core_from
        device = cycle_at * packers + block % packers
        column_pair = jnp.where(
            column_is_image,
            device * pair_rows + column_at,
            jnp.where(
                jnp.logical_and(column_is_slot, codes >= 0), cycle_at * group_rows + codes, -1
            ),
        )
        live = jnp.logical_and(
            jnp.logical_and(own_pair >= 0, column_pair >= 0), own_is_image != column_is_image
        )
        products = lax.dot_general(
            own16, rows, (((1,), (1,)), ((), ())), preferred_element_type=jnp.float32
        )
        logits = logit_scale * products + logit_shift
        signed = jnp.where(own_pair == column_pair, -logits, logits)
        small = jnp.exp(-jnp.abs(signed))
        softplus = jnp.maximum(signed, 0.0) + jnp.log1p(small)
        sigmoid = jnp.where(signed >= 0.0, 1.0, small) / (1.0 + small)
        loss = loss + jnp.sum(jnp.where(live, softplus, 0.0), axis=1, keepdims=True)
        weights = jnp.where(own_pair == column_pair, -sigmoid, sigmoid)
        weights = jnp.where(live, weights, 0.0).astype(jnp.bfloat16)
        upstream = upstream + jnp.dot(weights, rows, preferred_element_type=jnp.float32)
        return loss, upstream

    totals = (jnp.zeros((ROWS, 1), jnp.float32), jnp.zeros((ROWS, width), jnp.float32))
    for rows_ref, core_from in ((mine_ref, core_me), (other_ref, 1 - core_me)):
        work = functools.partial(one_chunk, rows_ref, core_from)
        chunks = devices // 2 // CHUNK
        totals = work(0, totals) if chunks == 1 else lax.fori_loop(0, chunks, work, totals)
    loss, upstream = totals

    upstream = logit_scale * upstream
    grads = own_inv * (upstream - own * jnp.sum(own * upstream, axis=-1, keepdims=True))
    loss = loss / (devices * pair_rows)
    lanes = lax.broadcasted_iota(jnp.int32, (1, pair_rows), 1)
    losses = jnp.zeros((1, pair_rows), jnp.float32)
    for row in range(pair_rows):
        losses = jnp.where(lanes == row, loss[row : row + 1, :], losses)
    loss_ref[...] = losses
    grad_images_ref[...] = grads[:pair_rows]
    grad_captions_ref[...] = jnp.where(own_pair >= 0, grads, 0.0)[pair_rows : pair_rows + slots]


def body(images, captions, caption_owner, caption_count, log_scale, bias):
    pair_rows, width = images.shape
    slots = captions.shape[0]
    packers = lax.axis_size("pack")
    chips = lax.axis_size("chip")
    receivers = chips * packers
    assert pair_rows + slots < ROWS and slots <= 128 and pair_rows * packers <= 256
    assert receivers % CHUNK == 0
    where = jnp.stack([lax.axis_index("chip"), lax.axis_index("core"), lax.axis_index("pack")])
    vmem = pl.BlockSpec(memory_space=pltpu.VMEM)
    smem = pl.BlockSpec(memory_space=pltpu.SMEM)
    sent = pl.pallas_call(
        pack_kernel,
        out_shape=jax.ShapeDtypeStruct((receivers * ROWS, width), jnp.bfloat16),
        in_specs=[vmem, vmem, smem, smem],
        out_specs=vmem,
    )(images, captions, caption_owner, caption_count)
    mine = lax.all_to_all(sent, ("chip", "pack"), split_axis=0, concat_axis=0, tiled=True)
    other = lax.ppermute(mine, "core", [(0, 1), (1, 0)])
    row_loss, grad_images, grad_captions = pl.pallas_call(
        functools.partial(pair_kernel, chips, packers),
        out_shape=(
            jax.ShapeDtypeStruct((1, pair_rows), jnp.float32),
            jax.ShapeDtypeStruct(images.shape, jnp.float32),
            jax.ShapeDtypeStruct(captions.shape, jnp.float32),
        ),
        in_specs=[smem] * 5 + [vmem] * 4,
        out_specs=(vmem, vmem, vmem),
        compiler_params=pltpu.CompilerParams(vmem_limit_bytes=32 * 1024 * 1024),
    )(where, caption_owner, caption_count, log_scale, bias, images, captions, mine, other)
    return row_loss.reshape(pair_rows), grad_images, grad_captions


def solution(mesh):
    cycles, packers = mesh.devices.shape
    split = Mesh(mesh.devices.reshape(cycles // 2, 2, packers), ("chip", "core", "pack"))
    rows = P(("chip", "core", "pack"))
    return jax.shard_map(
        body,
        mesh=split,
        in_specs=(rows, rows, rows, rows, P(), P()),
        out_specs=(rows, rows, rows),
        check_vma=False,
    )
```

time: 113 us -> 26.1 us (0.23)
  waiting for transfers between devices: 32.4 us -> 0.15 us
  blocking collectives: 46.9 us -> 19 us
  between operations: 17.4 us -> 2.62 us
  starting transfers between devices: 5.17 us -> 0.01 us
  local copies, waits for them, and re-layouts: 4.56 us -> 0.43 us
  Pallas kernels: 0 us -> 3.46 us
  other arithmetic: 3.14 us -> 0.08 us
  matrix products: 2.41 us -> 0 us
    unnamed x2 -> x0, waiting for transfers between devices: 32.4 us -> none
    all_gather x3 -> x0, blocking collectives: 31.1 us -> none  [the longest x1 14.2 us: body(): column_texts = lax.all_gather(text16, 'dp', axis=0, tiled=True)]
    all_to_all x0 -> x1, blocking collectives: none -> 19 us  [body(): lax.all_to_all(sent, ('chip', 'pack'), split_axis=0, concat_axis=0, tiled...]
    unnamed x1 -> x0, blocking collectives: 15.8 us -> none
    all_to_all x1 -> x0, starting transfers between devices: 5.16 us -> none  [body(): lax.all_to_all(outgoing.reshape(packers, pair_rows, outgoing.shape[1]), '...]
    unnamed x16 -> x6, local copies, waits for them, and re-layouts: 3.93 us -> 0.43 us
    pallas_call x0 -> x2, Pallas kernels: none -> 3.46 us  [the longest x1 1.82 us: body(): pl.pallas_call(functools.partial(pair_kernel, chips, packers), out_shape=...]
    dot_general x5 -> x0, matrix products: 2.41 us -> none  [the longest x1 0.9 us: body(): lax.dot_general(score_weights, image_rows, (((0,), (0,)), ((), ())), pref...]
  transfers between devices with their start and end apart: 2 -> 1, of which waited for: 1 -> 1; matrix products, arithmetic and copies ran while one was open for 3% -> 0% of each run, Pallas kernels for 0% -> 0%
where the time goes in v1:
time: 26.1 us; the launch traced here: 25.7 us
  blocking collectives  19 us (73%)
  Pallas kernels  3.46 us (13%)
  between operations  2.62 us (10%)
  local copies, waits for them, and re-layouts  0.43 us (2%)
    all_to_all x1, blocking collectives, body(): lax.all_to_all(sent, ('chip', 'pack'), split_axis=0, concat_axis=0, tiled...  19 us
    pallas_call x1, Pallas kernels, body(): pl.pallas_call(functools.partial(pair_kernel, chips, packers), out_shape=...  1.82 us
    pallas_call x1, Pallas kernels, body(): pl.pallas_call(pack_kernel, out_shape=jax.ShapeDtypeStruct((receivers * R...  1.64 us
  transfers between devices with their start and end apart: 1, of which 1 were waited for; matrix products, arithmetic and copies ran while one was open for 0% of the time, Pallas kernels for 0%

profile of v1, /device:TPU:0, one launch (start us, length us, event | category | flops | bytes accessed | tf_op | source)
XLA Modules:
  0.0 25.7 jit_solution(11018248782970196841)
XLA Ops:
  1.3 1.6 %shard_map.85 = bf16[128,1152]{1,0:T(8,128)(2,1)} custom-call(bf16[2,1152]{1,0:T(2,128)(2,1)} %images_ref.3, bf16[4,1152]{1,0:T(4,128)(2,1)} %captions_ref.3, s32[4]{0:T(128)} %owner_ref.3, s32[1]{0:T(128)S(6)} %copy.9.count_ref), custom_call_target="tpu_custom_call" | custom-call | tf_op jit(solution)/shard_map/pallas_call | solution.py:160
  2.9 19.0 %all_to_all.11 = bf16[16,8,1152]{2,1,0:T(8,128)(2,1)S(1)} all-to-all(bf16[16,8,1152]{2,1,0:T(8,128)(2,1)} %bitcast.8), channel_id=1, replica_groups=mesh['chip'=4,'core'=2,'pack'=4] {'chip','pack'}, dimensions={0} | all-to-all | bytes 589824 | tf_op jit(solution)/shard_map/all_to_all | solution.py:166
  21.9 0.0 collective-permute-start
  21.9 0.0 copy-start
  22.6 0.0 copy-start.1
  23.2 0.0 copy-start.2
  23.3 0.1 pad_add_fusion.where_ref
  23.3 0.2 collective-permute-done.other_ref
  23.5 0.0 copy-done
  23.5 0.0 copy-done.1
  23.5 0.4 %copy-done.2 = s32[4]{0:T(128)S(1)} copy-done((s32[4]{0:T(128)S(1)}, s32[4]{0:T(128)}, u32[]{:S(2)}) %copy-start.2) | copy-done | bytes 40
  23.9 1.8 %shard_map.86 = (f32[1,2]{1,0:T(1,128)}, f32[2,1152]{1,0:T(2,128)}, f32[4,1152]{1,0:T(4,128)}) custom-call(s32[3]{0:T(128)S(1)} %pad_add_fusion.where_ref, s32[4]{0:T(128)S(1)} %copy-done.2, s32[1]{0:T(128)S(6)} %copy.9.count_ref, f32[1]{0:T(128)S(6)} %copy.10.scale_ref, f32[1]{0:T(128)S(6)} %copy.11.bias_ref, bf16[2,1152]{1,0:T(2,128)(2,1)S(1)} %copy-done.1, ...), custom_call_target="tpu_custom_call" | custom-call | tf_op jit(solution)/shard_map/pallas_call | solution.py:168
Async XLA Ops:
  21.9 1.6 %collective-permute-start = (bf16[128,1152]{1,0:T(8,128)(2,1)S(1)}, bf16[128,1152]{1,0:T(8,128)(2,1)S(1)}, u32[]{:S(2)}, u32[]{:S(2)}) collective-permute-start(bf16[128,1152]{1,0:T(8,128)(2,1)S(1)} %bitcast.6), channel_id=1, source_target_pairs={{0,4},{4,0},{1,5},{5,1},{2,6},{6,2},{3,7},{7,3},{8,12},{12,8},{9,1... | collective-permute-start | bytes 884744 | tf_op jit(solution)/shard_map/ppermute | solution.py:167
  21.9 1.6 %copy-start = (bf16[4,1152]{1,0:T(4,128)(2,1)S(1)}, bf16[4,1152]{1,0:T(4,128)(2,1)}, u32[]{:S(2)}) copy-start(bf16[4,1152]{1,0:T(4,128)(2,1)} %captions_ref.3) | copy-start | bytes 27652
  22.6 0.9 %copy-start.1 = (bf16[2,1152]{1,0:T(2,128)(2,1)S(1)}, bf16[2,1152]{1,0:T(2,128)(2,1)}, u32[]{:S(2)}) copy-start(bf16[2,1152]{1,0:T(2,128)(2,1)} %images_ref.3) | copy-start | bytes 13828
  23.2 0.7 %copy-start.2 = (s32[4]{0:T(128)S(1)}, s32[4]{0:T(128)}, u32[]{:S(2)}) copy-start(s32[4]{0:T(128)} %owner_ref.3) | copy-start | bytes 52

commit v2 on v1

--- a/solution.py
+++ b/solution.py
@@ -11,6 +11,7 @@
 eps = 1e-06
 ROWS = 8
 CHUNK = 16
+APART = {"chip": (2, 3, 1), "pack": (3, 1, 2)}
 
 
 def unit_rows(rows):
@@ -19,69 +20,70 @@
     return floats * inverse, inverse
 
 
-def pack_kernel(images_ref, captions_ref, owner_ref, count_ref, sent_ref):
+def pack_kernel(images_ref, captions_ref, owner_ref, count_ref, sent_ref, own_ref, aside_ref):
+    pair_rows = images_ref.shape[0]
     slots, width = captions_ref.shape
-    images, _ = unit_rows(images_ref[...])
-    captions, _ = unit_rows(captions_ref[...])
-    left = ROWS - images_ref.shape[0] - slots
-    lanes = lax.broadcasted_iota(jnp.int32, (left, width), 1)
-    codes = jnp.zeros((left, width), jnp.float32)
+    owner = owner_ref[...].reshape(1, slots).astype(jnp.float32)
+    count = count_ref[0]
+    left = ROWS - pair_rows - slots
+    images, images_inv = unit_rows(images_ref[...])
+    captions, captions_inv = unit_rows(captions_ref[...])
+    codes = [jnp.where(slot < count, owner[:, slot : slot + 1], -1.0) for slot in range(slots)]
+    own = jnp.concatenate([images, captions, jnp.zeros((left, width), jnp.float32)], axis=0)
+    own_ref[...] = own
+    own_inv = jnp.concatenate([images_inv, captions_inv, jnp.zeros((left, 1), jnp.float32)], axis=0)
+    rows = lax.broadcasted_iota(jnp.int32, (ROWS, 128), 0)
+    lanes = lax.broadcasted_iota(jnp.int32, (ROWS, 128), 1)
+    aside = jnp.where(lanes == 0, own_inv, 0.0)
     for slot in range(slots):
-        code = jnp.where(slot < count_ref[0], owner_ref[slot], -1).astype(jnp.float32)
-        codes = jnp.where(lanes == slot, code, codes)
-    block = jnp.concatenate([images, captions, codes], axis=0).astype(jnp.bfloat16)
-
-    def put(receiver):
-        sent_ref[pl.ds(receiver * ROWS, ROWS), :] = block
-
-    receivers = sent_ref.shape[0] // ROWS
-    if receivers <= 16:
-        for receiver in range(receivers):
-            put(receiver)
-    else:
-        pl.loop(0, receivers)(put)
+        aside = jnp.where(jnp.logical_and(lanes == 1, rows == pair_rows + slot), codes[slot], aside)
+    aside_ref[...] = aside
+    front = own[:, :128]
+    for slot in range(slots):
+        here = jnp.logical_and(lanes == slot, rows == pair_rows + slots)
+        front = jnp.where(here, codes[slot], front)
+    block = jnp.concatenate([front, own[:, 128:]], axis=1)
+    sent_ref[...] = block.astype(jnp.bfloat16)
 
 
 def pair_kernel(
     chips,
     packers,
-    where_ref,
-    owner_ref,
-    count_ref,
+    pair_rows,
+    slots,
     scale_ref,
     bias_ref,
-    images_ref,
-    captions_ref,
+    own_ref,
+    aside_ref,
     mine_ref,
     other_ref,
     loss_ref,
     grad_images_ref,
     grad_captions_ref,
 ):
-    pair_rows = images_ref.shape[0]
-    slots, width = captions_ref.shape
+    width = own_ref.shape[1]
     group_rows = pair_rows * packers
-    chip_me, core_me, pack_me = where_ref[0], where_ref[1], where_ref[2]
+    chip_me, core_me, pack_me = lax.axis_index("chip"), lax.axis_index("core"), lax.axis_index("pack")
     cycle_me = chip_me * 2 + core_me
     me = cycle_me * packers + pack_me
     devices = chips * 2 * packers
     chunk_rows = CHUNK * ROWS
+
+    own = own_ref[...]
+    own16 = own.astype(jnp.bfloat16)
+    aside = aside_ref[...]
+    own_inv, own_codes = aside[:, 0:1], aside[:, 1:2].astype(jnp.int32)
     logit_scale = jnp.exp(jnp.full((1, 1), scale_ref[0], jnp.float32))
     logit_shift = bias_ref[0]
 
-    images, images_inv = unit_rows(images_ref[...])
-    captions, captions_inv = unit_rows(captions_ref[...])
-    filler = jnp.zeros((ROWS - pair_rows - slots, width), jnp.float32)
-    own = jnp.concatenate([images, captions, filler], axis=0)
-    own_inv = jnp.concatenate([images_inv, captions_inv, filler[:, :1]], axis=0)
-    own16 = own.astype(jnp.bfloat16)
-
     own_at = lax.broadcasted_iota(jnp.int32, (ROWS, 1), 0)
-    own_pair = jnp.where(own_at < pair_rows, me * pair_rows + own_at, -1)
-    for slot in range(slots):
-        pair = jnp.where(slot < count_ref[0], cycle_me * group_rows + owner_ref[slot], -1)
-        own_pair = jnp.where(own_at == pair_rows + slot, pair, own_pair)
     own_is_image = own_at < pair_rows
+    own_is_slot = jnp.logical_and(own_at >= pair_rows, own_at < pair_rows + slots)
+    own_pair = jnp.where(
+        own_is_image,
+        me * pair_rows + own_at,
+        jnp.where(jnp.logical_and(own_is_slot, own_codes >= 0), cycle_me * group_rows + own_codes, -1),
+    )
 
     column = lax.broadcasted_iota(jnp.int32, (1, chunk_rows), 1)
     column_at = column % ROWS
@@ -101,8 +103,9 @@
         codes = jnp.dot(rows[:, :128], spread, preferred_element_type=jnp.float32)
         codes = jnp.sum(jnp.where(code_here, codes, 0.0), axis=0, keepdims=True).astype(jnp.int32)
         block = chunk * CHUNK + column // ROWS
-        cycle_at = block // packers * 2 + core_from
-        device = cycle_at * packers + block % packers
+        chip_at, core_at, pack_at = source(block, chip_me, core_from, pack_me, chips, packers)
+        cycle_at = chip_at * 2 + core_at
+        device = cycle_at * packers + pack_at
         column_pair = jnp.where(
             column_is_image,
             device * pair_rows + column_at,
@@ -146,36 +149,71 @@
     grad_captions_ref[...] = jnp.where(own_pair >= 0, grads, 0.0)[pair_rows : pair_rows + slots]
 
 
+def gather(rows):
+    chips, packers = lax.axis_size("chip"), lax.axis_size("pack")
+    if chips != 4 or packers != 4:
+        return lax.all_gather(lax.all_gather(rows, "chip", axis=0, tiled=True), "pack", axis=0, tiled=True)
+    for axis, distances in APART.items():
+        taken = [rows]
+        for apart in distances:
+            pairs = []
+            for chip in range(4):
+                for core in range(2):
+                    for pack in range(4):
+                        peer_chip = chip ^ apart if axis == "chip" else chip
+                        peer_pack = pack ^ apart if axis == "pack" else pack
+                        peer = (peer_chip * 2 + 1 - core) * 4 + peer_pack
+                        pairs.append(((chip * 2 + core) * 4 + pack, peer))
+            taken.append(lax.ppermute(rows, ("chip", "core", "pack"), pairs))
+        rows = jnp.concatenate(taken, axis=0)
+    return rows
+
+
+def source(block, chip_me, core_me, pack_me, chips, packers):
+    if chips != 4 or packers != 4:
+        return block % chips, core_me, block // chips
+    chip, core, pack = chip_me, core_me, pack_me
+    for at, apart in enumerate(APART["chip"]):
+        here = block % 4 == at + 1
+        chip, core = jnp.where(here, chip_me ^ apart, chip), jnp.where(here, 1 - core, core)
+    for at, apart in enumerate(APART["pack"]):
+        here = block // 4 == at + 1
+        pack, core = jnp.where(here, pack_me ^ apart, pack), jnp.where(here, 1 - core, core)
+    return chip, core, pack
+
+
 def body(images, captions, caption_owner, caption_count, log_scale, bias):
     pair_rows, width = images.shape
     slots = captions.shape[0]
     packers = lax.axis_size("pack")
     chips = lax.axis_size("chip")
-    receivers = chips * packers
     assert pair_rows + slots < ROWS and slots <= 128 and pair_rows * packers <= 256
-    assert receivers % CHUNK == 0
-    where = jnp.stack([lax.axis_index("chip"), lax.axis_index("core"), lax.axis_index("pack")])
+    assert chips * packers % CHUNK == 0
     vmem = pl.BlockSpec(memory_space=pltpu.VMEM)
     smem = pl.BlockSpec(memory_space=pltpu.SMEM)
-    sent = pl.pallas_call(
+    sent, own, aside = pl.pallas_call(
         pack_kernel,
-        out_shape=jax.ShapeDtypeStruct((receivers * ROWS, width), jnp.bfloat16),
-        in_specs=[vmem, vmem, smem, smem],
-        out_specs=vmem,
+        out_shape=(
+            pltpu.VMEM((ROWS, width), jnp.bfloat16),
+            pltpu.VMEM((ROWS, width), jnp.float32),
+            pltpu.VMEM((ROWS, 128), jnp.float32),
+        ),
+        in_specs=[vmem, vmem, vmem, smem],
+        out_specs=(vmem, vmem, vmem),
     )(images, captions, caption_owner, caption_count)
-    mine = lax.all_to_all(sent, ("chip", "pack"), split_axis=0, concat_axis=0, tiled=True)
+    mine = gather(sent)
     other = lax.ppermute(mine, "core", [(0, 1), (1, 0)])
     row_loss, grad_images, grad_captions = pl.pallas_call(
-        functools.partial(pair_kernel, chips, packers),
+        functools.partial(pair_kernel, chips, packers, pair_rows, slots),
         out_shape=(
             jax.ShapeDtypeStruct((1, pair_rows), jnp.float32),
             jax.ShapeDtypeStruct(images.shape, jnp.float32),
             jax.ShapeDtypeStruct(captions.shape, jnp.float32),
         ),
-        in_specs=[smem] * 5 + [vmem] * 4,
+        in_specs=[smem] * 2 + [vmem] * 4,
         out_specs=(vmem, vmem, vmem),
         compiler_params=pltpu.CompilerParams(vmem_limit_bytes=32 * 1024 * 1024),
-    )(where, caption_owner, caption_count, log_scale, bias, images, captions, mine, other)
+    )(log_scale, bias, own, aside, mine, other)
     return row_loss.reshape(pair_rows), grad_images, grad_captions
 
 

time: 26.1 us -> 21.2 us (0.81)
  blocking collectives: 19 us -> 0 us
  starting transfers between devices: 0.01 us -> 9.12 us
  waiting for transfers between devices: 0.15 us -> 7.09 us
  Pallas kernels: 3.46 us -> 2.11 us
  local copies, waits for them, and re-layouts: 0.43 us -> 0.07 us
    all_to_all x1 -> x0, blocking collectives: 19 us -> none  [body(): lax.all_to_all(sent, ('chip', 'pack'), split_axis=0, concat_axis=0, tiled...]
    ppermute x0 -> x6, starting transfers between devices: none -> 8.97 us  [gather(): taken.append(lax.ppermute(rows, ('chip', 'core', 'pack'), pairs))]
    ppermute x0 -> x6, waiting for transfers between devices: none -> 6.9 us  [gather(): taken.append(lax.ppermute(rows, ('chip', 'core', 'pack'), pairs))]
    pallas_call x2, Pallas kernels: 3.46 us -> 2.11 us  [the longest x1 1.23 us: body(): pl.pallas_call(functools.partial(pair_kernel, chips, packers, pair_rows,...]
    unnamed x6 -> x5, local copies, waits for them, and re-layouts: 0.43 us -> 0.05 us
  transfers between devices with their start and end apart: 1 -> 7, of which waited for: 1 -> 4; matrix products, arithmetic and copies ran while one was open for 0% -> 0% of each run, Pallas kernels for 0% -> 0%
where the time goes in v2:
time: 21.2 us; the launch traced here: 21 us
  starting transfers between devices  9.12 us (43%)
  waiting for transfers between devices  7.09 us (33%)
  between operations  2.6 us (12%)
  Pallas kernels  2.11 us (10%)
    ppermute x6, starting transfers between devices, gather(): taken.append(lax.ppermute(rows, ('chip', 'core', 'pack'), pairs))  8.97 us
    ppermute x6, waiting for transfers between devices, gather(): taken.append(lax.ppermute(rows, ('chip', 'core', 'pack'), pairs))  6.9 us
    pallas_call x1, Pallas kernels, body(): pl.pallas_call(functools.partial(pair_kernel, chips, packers, pair_rows,...  1.23 us
    pallas_call x1, Pallas kernels, body(): pl.pallas_call(pack_kernel, out_shape=(pltpu.VMEM((ROWS, width), jnp.bflo...  0.88 us
  transfers between devices with their start and end apart: 7, of which 4 were waited for; matrix products, arithmetic and copies ran while one was open for 0% of the time, Pallas kernels for 0%

profile of v2, /device:TPU:0, one launch (start us, length us, event | category | flops | bytes accessed | tf_op | source)
XLA Modules:
  0.0 21.0 jit_solution(2166938566949574765)
XLA Ops:
  1.3 0.9 %shard_map.85 = (bf16[8,1152]{1,0:T(8,128)(2,1)S(1)}, f32[8,1152]{1,0:T(8,128)S(1)}, f32[8,128]{1,0:T(8,128)S(1)}) custom-call(bf16[2,1152]{1,0:T(2,128)(2,1)} %images_ref.1, bf16[4,1152]{1,0:T(4,128)(2,1)} %captions_ref.1, s32[4]{0:T(128)} %owner_ref.1, s32[1]{0:T(128)S(6)} %copy.18.count_ref), custom_call_target="tpu_custom_call" | custom-call | tf_op jit(solution)/shard_map/pallas_call | solution.py:194
  2.2 3.5 %collective-permute-start = (bf16[8,1152]{1,0:T(8,128)(2,1)S(1)}, bf16[8,1152]{1,0:T(8,128)(2,1)S(1)}, u32[]{:S(2)}, u32[]{:S(2)}) collective-permute-start(bf16[8,1152]{1,0:T(8,128)(2,1)S(1)} %get-tuple-element.11), channel_id=1, source_target_pairs={{0,20},{1,21},{2,22},{3,23},{4,16},{5,17},{6,18},{7,19},{8,28},{9,... | collective-permute-start | bytes 55304 | tf_op jit(solution)/shard_map/ppermute | solution.py:167
  5.7 1.6 %collective-permute-start.1 = (bf16[8,1152]{1,0:T(8,128)(2,1)S(1)}, bf16[8,1152]{1,0:T(8,128)(2,1)S(1)}, u32[]{:S(2)}, u32[]{:S(2)}) collective-permute-start(bf16[8,1152]{1,0:T(8,128)(2,1)S(1)} %get-tuple-element.11), channel_id=1, source_target_pairs={{0,28},{1,29},{2,30},{3,31},{4,24},{5,25},{6,26},{7,27},{8,20},{9,... | collective-permute-start | bytes 55304 | tf_op jit(solution)/shard_map/ppermute | solution.py:167
  7.3 0.2 %collective-permute-start.2 = (bf16[8,1152]{1,0:T(8,128)(2,1)S(1)}, bf16[8,1152]{1,0:T(8,128)(2,1)S(1)}, u32[]{:S(2)}, u32[]{:S(2)}) collective-permute-start(bf16[8,1152]{1,0:T(8,128)(2,1)S(1)} %get-tuple-element.11), channel_id=1, source_target_pairs={{0,12},{1,13},{2,14},{3,15},{4,8},{5,9},{6,10},{7,11},{8,4},{9,5},... | collective-permute-start | bytes 55304 | tf_op jit(solution)/shard_map/ppermute | solution.py:167
  7.5 0.0 collective-permute-done
  7.5 3.1 %collective-permute-done.1 = bf16[8,1152]{1,0:T(8,128)(2,1)S(1)} collective-permute-done((bf16[8,1152]{1,0:T(8,128)(2,1)S(1)}, bf16[8,1152]{1,0:T(8,128)(2,1)S(1)}, u32[]{:S(2)}, u32[]{:S(2)}) %collective-permute-start.1) | collective-permute-done | bytes 18464 | tf_op jit(solution)/shard_map/ppermute | solution.py:167
  10.7 0.0 collective-permute-done.2
  10.7 2.9 %collective-permute-start.3 = (bf16[32,1152]{1,0:T(8,128)(2,1)S(1)}, bf16[32,1152]{1,0:T(8,128)(2,1)S(1)}, u32[]{:S(2)}, u32[]{:S(2)}) collective-permute-start(bf16[32,1152]{1,0:T(8,128)(2,1)S(1)} %get-tuple-element.15), channel_id=1, source_target_pairs={{0,7},{1,6},{2,5},{3,4},{4,3},{5,2},{6,1},{7,0},{8,15},{9,14},{10,... | collective-permute-start | bytes 221192 | tf_op jit(solution)/shard_map/ppermute | solution.py:167
  13.6 0.0 collective-permute-start.4
  13.6 0.8 %collective-permute-start.5 = (bf16[32,1152]{1,0:T(8,128)(2,1)S(1)}, bf16[32,1152]{1,0:T(8,128)(2,1)S(1)}, u32[]{:S(2)}, u32[]{:S(2)}) collective-permute-start(bf16[32,1152]{1,0:T(8,128)(2,1)S(1)} %get-tuple-element.15), channel_id=1, source_target_pairs={{0,6},{1,7},{2,4},{3,5},{4,2},{5,3},{6,0},{7,1},{8,14},{9,15},{10,... | collective-permute-start | bytes 221192 | tf_op jit(solution)/shard_map/ppermute | solution.py:167
  14.3 1.9 %collective-permute-done.3 = bf16[32,1152]{1,0:T(8,128)(2,1)S(1)} collective-permute-done((bf16[32,1152]{1,0:T(8,128)(2,1)S(1)}, bf16[32,1152]{1,0:T(8,128)(2,1)S(1)}, u32[]{:S(2)}, u32[]{:S(2)}) %collective-permute-start.3) | collective-permute-done | bytes 73760 | tf_op jit(solution)/shard_map/ppermute | solution.py:167
  16.2 1.9 %collective-permute-done.4 = bf16[32,1152]{1,0:T(8,128)(2,1)S(1)} collective-permute-done((bf16[32,1152]{1,0:T(8,128)(2,1)S(1)}, bf16[32,1152]{1,0:T(8,128)(2,1)S(1)}, u32[]{:S(2)}, u32[]{:S(2)}) %collective-permute-start.4) | collective-permute-done | bytes 73760 | tf_op jit(solution)/shard_map/ppermute | solution.py:167
  18.1 0.0 collective-permute-done.5
  18.1 0.2 collective-permute-start.6
  19.6 0.2 collective-permute-done.6.other_ref
  19.8 1.2 %shard_map.86 = (f32[1,2]{1,0:T(1,128)}, f32[2,1152]{1,0:T(2,128)}, f32[4,1152]{1,0:T(4,128)}) custom-call(f32[1]{0:T(128)S(6)} %copy.19.scale_ref, f32[1]{0:T(128)S(6)} %copy.20.bias_ref, f32[8,1152]{1,0:T(8,128)S(1)} %get-tuple-element.9.own_ref, f32[8,128]{1,0:T(8,128)S(1)} %get-tuple-element.10.aside_ref, ...), custom_call_target="tpu_custom_call" | custom-call | tf_op jit(solution)/shard_map/pallas_call | solution.py:206
  (7 shorter events, 0.1 us)
Async XLA Ops:
  2.2 5.4 %collective-permute-start = (bf16[8,1152]{1,0:T(8,128)(2,1)S(1)}, bf16[8,1152]{1,0:T(8,128)(2,1)S(1)}, u32[]{:S(2)}, u32[]{:S(2)}) collective-permute-start(bf16[8,1152]{1,0:T(8,128)(2,1)S(1)} %get-tuple-element.11), channel_id=1, source_target_pairs={{0,20},{1,21},{2,22},{3,23},{4,16},{5,17},{6,18},{7,19},{8,28},{9,... | collective-permute-start | bytes 55304 | tf_op jit(solution)/shard_map/ppermute | solution.py:167
  5.7 5.0 %collective-permute-start.1 = (bf16[8,1152]{1,0:T(8,128)(2,1)S(1)}, bf16[8,1152]{1,0:T(8,128)(2,1)S(1)}, u32[]{:S(2)}, u32[]{:S(2)}) collective-permute-start(bf16[8,1152]{1,0:T(8,128)(2,1)S(1)} %get-tuple-element.11), channel_id=1, source_target_pairs={{0,28},{1,29},{2,30},{3,31},{4,24},{5,25},{6,26},{7,27},{8,20},{9,... | collective-permute-start | bytes 55304 | tf_op jit(solution)/shard_map/ppermute | solution.py:167
  7.3 3.4 %collective-permute-start.2 = (bf16[8,1152]{1,0:T(8,128)(2,1)S(1)}, bf16[8,1152]{1,0:T(8,128)(2,1)S(1)}, u32[]{:S(2)}, u32[]{:S(2)}) collective-permute-start(bf16[8,1152]{1,0:T(8,128)(2,1)S(1)} %get-tuple-element.11), channel_id=1, source_target_pairs={{0,12},{1,13},{2,14},{3,15},{4,8},{5,9},{6,10},{7,11},{8,4},{9,5},... | collective-permute-start | bytes 55304 | tf_op jit(solution)/shard_map/ppermute | solution.py:167
  10.7 5.5 %collective-permute-start.3 = (bf16[32,1152]{1,0:T(8,128)(2,1)S(1)}, bf16[32,1152]{1,0:T(8,128)(2,1)S(1)}, u32[]{:S(2)}, u32[]{:S(2)}) collective-permute-start(bf16[32,1152]{1,0:T(8,128)(2,1)S(1)} %get-tuple-element.15), channel_id=1, source_target_pairs={{0,7},{1,6},{2,5},{3,4},{4,3},{5,2},{6,1},{7,0},{8,15},{9,14},{10,... | collective-permute-start | bytes 221192 | tf_op jit(solution)/shard_map/ppermute | solution.py:167
  13.6 4.5 %collective-permute-start.4 = (bf16[32,1152]{1,0:T(8,128)(2,1)S(1)}, bf16[32,1152]{1,0:T(8,128)(2,1)S(1)}, u32[]{:S(2)}, u32[]{:S(2)}) collective-permute-start(bf16[32,1152]{1,0:T(8,128)(2,1)S(1)} %get-tuple-element.15), channel_id=1, source_target_pairs={{0,5},{1,4},{2,7},{3,6},{4,1},{5,0},{6,3},{7,2},{8,13},{9,12},{10,... | collective-permute-start | bytes 221192 | tf_op jit(solution)/shard_map/ppermute | solution.py:167
  13.6 4.5 %collective-permute-start.5 = (bf16[32,1152]{1,0:T(8,128)(2,1)S(1)}, bf16[32,1152]{1,0:T(8,128)(2,1)S(1)}, u32[]{:S(2)}, u32[]{:S(2)}) collective-permute-start(bf16[32,1152]{1,0:T(8,128)(2,1)S(1)} %get-tuple-element.15), channel_id=1, source_target_pairs={{0,6},{1,7},{2,4},{3,5},{4,2},{5,3},{6,0},{7,1},{8,14},{9,15},{10,... | collective-permute-start | bytes 221192 | tf_op jit(solution)/shard_map/ppermute | solution.py:167
  18.1 1.6 %collective-permute-start.6 = (bf16[128,1152]{1,0:T(8,128)(2,1)S(1)}, bf16[128,1152]{1,0:T(8,128)(2,1)S(1)}, u32[]{:S(2)}, u32[]{:S(2)}) collective-permute-start(bf16[128,1152]{1,0:T(8,128)(2,1)S(1)} %constant_dynamic-update-slice_fusion.4.mine_ref), channel_id=1, source_target_pairs={{0,4},{4,0},{1,5},{5,1},{2,6},{6,2},{3,7},{7,3},{8,12},{12,8},{9,1... | collective-permute-start | bytes 884744 | tf_op jit(solution)/shard_map/ppermute | solution.py:205

commit v3 on v2

--- a/solution.py
+++ b/solution.py
@@ -9,9 +9,11 @@
 from jax.sharding import PartitionSpec as P
 
 eps = 1e-06
-ROWS = 8
+ROWS, SLOTS, PAIR_ROWS = 8, 4, 2
+HEAD, TAIL, PIECE = 896, 256, 640
+CODES = TAIL + HEAD + TAIL - PIECE
 CHUNK = 16
-APART = {"chip": (2, 3, 1), "pack": (3, 1, 2)}
+APART = {"chip": (2, 3, 1), "pack": (3, 2, 1)}
 
 
 def unit_rows(rows):
@@ -20,7 +22,7 @@
     return floats * inverse, inverse
 
 
-def pack_kernel(images_ref, captions_ref, owner_ref, count_ref, sent_ref, own_ref, aside_ref):
+def pack_kernel(images_ref, captions_ref, owner_ref, count_ref, sent_ref, own_ref, left_ref, aside_ref):
     pair_rows = images_ref.shape[0]
     slots, width = captions_ref.shape
     owner = owner_ref[...].reshape(1, slots).astype(jnp.float32)
@@ -38,30 +40,45 @@
     for slot in range(slots):
         aside = jnp.where(jnp.logical_and(lanes == 1, rows == pair_rows + slot), codes[slot], aside)
     aside_ref[...] = aside
-    front = own[:, :128]
+    is_image = lax.broadcasted_iota(jnp.int32, (ROWS, 1), 0) < pair_rows
+
+    def blank(lanes_left):
+        return jnp.zeros((ROWS, lanes_left), jnp.float32)
+
+    first = jnp.where(is_image, own[:, :HEAD], jnp.concatenate([blank(TAIL), own[:, :PIECE]], axis=1))
+    second = jnp.where(
+        is_image,
+        jnp.concatenate([own[:, HEAD:], blank(HEAD - TAIL)], axis=1),
+        jnp.concatenate([blank(TAIL), own[:, PIECE:], blank(HEAD - CODES)], axis=1),
+    )
+    left_ref[...] = jnp.concatenate([first, second], axis=0).astype(jnp.bfloat16)
+    code_lane = lax.broadcasted_iota(jnp.int32, (1, HEAD - CODES), 1)
+    code_row = jnp.zeros((1, HEAD - CODES), jnp.float32)
     for slot in range(slots):
-        here = jnp.logical_and(lanes == slot, rows == pair_rows + slots)
-        front = jnp.where(here, codes[slot], front)
-    block = jnp.concatenate([front, own[:, 128:]], axis=1)
-    sent_ref[...] = block.astype(jnp.bfloat16)
-
-
-def pair_kernel(
-    chips,
-    packers,
-    pair_rows,
-    slots,
-    scale_ref,
-    bias_ref,
-    own_ref,
-    aside_ref,
-    mine_ref,
-    other_ref,
-    loss_ref,
-    grad_images_ref,
-    grad_captions_ref,
-):
-    width = own_ref.shape[1]
+        code_row = jnp.where(code_lane == slot, codes[slot], code_row)
+    pieces = [
+        images[0:1, :PIECE],
+        jnp.concatenate([images[0:1, PIECE:], code_row], axis=1),
+        images[1:2, :PIECE],
+        jnp.concatenate([images[1:2, PIECE:], jnp.zeros_like(code_row)], axis=1),
+    ]
+    lower = jnp.concatenate([captions[:, HEAD:], jnp.concatenate(pieces, axis=0)], axis=1)
+    sent_ref[...] = jnp.concatenate([captions[:, :HEAD], lower], axis=0).astype(jnp.bfloat16)
+
+
+def scalars_kernel(scale_ref, bias_ref, sent_ref, near_ref, scalars_ref):
+    near_ref[...] = sent_ref[...]
+    lanes = lax.broadcasted_iota(jnp.int32, (ROWS, 128), 1)
+    scale = jnp.exp(jnp.full((ROWS, 128), scale_ref[0], jnp.float32))
+    scalars_ref[...] = jnp.where(lanes == 0, scale, bias_ref[0])
+
+
+def pair_kernel(chips, packers, pair_rows, slots, last, *refs):
+    if last:
+        left_ref, aside_ref, scalars_ref, rows_ref, own_ref, loss_in_ref, upstream_in_ref = refs[:7]
+        loss_ref, grad_images_ref, grad_captions_ref = refs[7:]
+    else:
+        left_ref, aside_ref, scalars_ref, rows_ref, loss_out_ref, upstream_out_ref = refs
     group_rows = pair_rows * packers
     chip_me, core_me, pack_me = lax.axis_index("chip"), lax.axis_index("core"), lax.axis_index("pack")
     cycle_me = chip_me * 2 + core_me
@@ -69,12 +86,10 @@
     devices = chips * 2 * packers
     chunk_rows = CHUNK * ROWS
 
-    own = own_ref[...]
-    own16 = own.astype(jnp.bfloat16)
+    left = left_ref[...]
     aside = aside_ref[...]
     own_inv, own_codes = aside[:, 0:1], aside[:, 1:2].astype(jnp.int32)
-    logit_scale = jnp.exp(jnp.full((1, 1), scale_ref[0], jnp.float32))
-    logit_shift = bias_ref[0]
+    logit_scale, logit_shift = scalars_ref[:, 0:1], scalars_ref[:, 1:2]
 
     own_at = lax.broadcasted_iota(jnp.int32, (ROWS, 1), 0)
     own_is_image = own_at < pair_rows
@@ -87,20 +102,21 @@
 
     column = lax.broadcasted_iota(jnp.int32, (1, chunk_rows), 1)
     column_at = column % ROWS
-    column_is_image = column_at < pair_rows
-    column_is_slot = jnp.logical_and(column_at >= pair_rows, column_at < pair_rows + slots)
+    column_is_image = jnp.logical_or(column_at == SLOTS, column_at == SLOTS + 2)
+    column_is_slot = column_at < SLOTS
+    lanes_left = HEAD - CODES
     spread = (
-        lax.broadcasted_iota(jnp.int32, (128, chunk_rows), 0)
-        == lax.broadcasted_iota(jnp.int32, (128, chunk_rows), 1) % ROWS - pair_rows
+        lax.broadcasted_iota(jnp.int32, (lanes_left, chunk_rows), 0)
+        == lax.broadcasted_iota(jnp.int32, (lanes_left, chunk_rows), 1) % ROWS
     ).astype(jnp.bfloat16)
     code_row = lax.broadcasted_iota(jnp.int32, (chunk_rows, chunk_rows), 0)
     code_column = lax.broadcasted_iota(jnp.int32, (chunk_rows, chunk_rows), 1)
-    code_here = code_row == code_column // ROWS * ROWS + pair_rows + slots
+    code_here = code_row == code_column // ROWS * ROWS + SLOTS + 1
 
     def one_chunk(rows_ref, core_from, chunk, totals):
         loss, upstream = totals
         rows = rows_ref[pl.ds(chunk * chunk_rows, chunk_rows), :]
-        codes = jnp.dot(rows[:, :128], spread, preferred_element_type=jnp.float32)
+        codes = jnp.dot(rows[:, CODES:], spread, preferred_element_type=jnp.float32)
         codes = jnp.sum(jnp.where(code_here, codes, 0.0), axis=0, keepdims=True).astype(jnp.int32)
         block = chunk * CHUNK + column // ROWS
         chip_at, core_at, pack_at = source(block, chip_me, core_from, pack_me, chips, packers)
@@ -108,7 +124,7 @@
         device = cycle_at * packers + pack_at
         column_pair = jnp.where(
             column_is_image,
-            device * pair_rows + column_at,
+            device * pair_rows + (column_at - SLOTS) // 2,
             jnp.where(
                 jnp.logical_and(column_is_slot, codes >= 0), cycle_at * group_rows + codes, -1
             ),
@@ -117,27 +133,44 @@
             jnp.logical_and(own_pair >= 0, column_pair >= 0), own_is_image != column_is_image
         )
         products = lax.dot_general(
-            own16, rows, (((1,), (1,)), ((), ())), preferred_element_type=jnp.float32
-        )
-        logits = logit_scale * products + logit_shift
+            left, rows, (((1,), (1,)), ((), ())), preferred_element_type=jnp.float32
+        )
+        second = products[ROWS:]
+        second = jnp.where(
+            own_is_image, pltpu.roll(second, chunk_rows - SLOTS, 1), pltpu.roll(second, chunk_rows - 1, 1)
+        )
+        logits = logit_scale * (products[:ROWS] + second) + logit_shift
         signed = jnp.where(own_pair == column_pair, -logits, logits)
         small = jnp.exp(-jnp.abs(signed))
         softplus = jnp.maximum(signed, 0.0) + jnp.log1p(small)
         sigmoid = jnp.where(signed >= 0.0, 1.0, small) / (1.0 + small)
         loss = loss + jnp.sum(jnp.where(live, softplus, 0.0), axis=1, keepdims=True)
         weights = jnp.where(own_pair == column_pair, -sigmoid, sigmoid)
-        weights = jnp.where(live, weights, 0.0).astype(jnp.bfloat16)
+        weights = jnp.where(live, weights, 0.0)
+        second = jnp.where(own_is_image, pltpu.roll(weights, SLOTS, 1), pltpu.roll(weights, 1, 1))
+        weights = jnp.concatenate([weights, second], axis=0).astype(jnp.bfloat16)
         upstream = upstream + jnp.dot(weights, rows, preferred_element_type=jnp.float32)
         return loss, upstream
 
-    totals = (jnp.zeros((ROWS, 1), jnp.float32), jnp.zeros((ROWS, width), jnp.float32))
-    for rows_ref, core_from in ((mine_ref, core_me), (other_ref, 1 - core_me)):
-        work = functools.partial(one_chunk, rows_ref, core_from)
-        chunks = devices // 2 // CHUNK
-        totals = work(0, totals) if chunks == 1 else lax.fori_loop(0, chunks, work, totals)
-    loss, upstream = totals
-
-    upstream = logit_scale * upstream
+    if last:
+        totals = (loss_in_ref[:, 0:1], upstream_in_ref[...])
+    else:
+        totals = (jnp.zeros((ROWS, 1), jnp.float32), jnp.zeros((2 * ROWS, HEAD), jnp.float32))
+    work = functools.partial(one_chunk, rows_ref, 1 - core_me if last else core_me)
+    chunks = devices // 2 // CHUNK
+    loss, upstream = work(0, totals) if chunks == 1 else lax.fori_loop(0, chunks, work, totals)
+    if not last:
+        loss_out_ref[...] = jnp.broadcast_to(loss, (ROWS, 128))
+        upstream_out_ref[...] = upstream
+        return
+
+    own = own_ref[...]
+    first, second = upstream[:ROWS], upstream[ROWS:]
+    upstream = logit_scale * jnp.where(
+        own_is_image,
+        jnp.concatenate([first, second[:, :TAIL]], axis=1),
+        jnp.concatenate([first[:, TAIL:], second[:, TAIL:CODES]], axis=1),
+    )
     grads = own_inv * (upstream - own * jnp.sum(own * upstream, axis=-1, keepdims=True))
     loss = loss / (devices * pair_rows)
     lanes = lax.broadcasted_iota(jnp.int32, (1, pair_rows), 1)
@@ -149,12 +182,12 @@
     grad_captions_ref[...] = jnp.where(own_pair >= 0, grads, 0.0)[pair_rows : pair_rows + slots]
 
 
-def gather(rows):
+def gather(rows, near):
     chips, packers = lax.axis_size("chip"), lax.axis_size("pack")
     if chips != 4 or packers != 4:
         return lax.all_gather(lax.all_gather(rows, "chip", axis=0, tiled=True), "pack", axis=0, tiled=True)
     for axis, distances in APART.items():
-        taken = [rows]
+        taken = [near if axis == "chip" else rows]
         for apart in distances:
             pairs = []
             for chip in range(4):
@@ -187,33 +220,50 @@
     slots = captions.shape[0]
     packers = lax.axis_size("pack")
     chips = lax.axis_size("chip")
-    assert pair_rows + slots < ROWS and slots <= 128 and pair_rows * packers <= 256
+    assert (pair_rows, slots, width) == (PAIR_ROWS, SLOTS, HEAD + TAIL) and pair_rows * packers <= 256
     assert chips * packers % CHUNK == 0
     vmem = pl.BlockSpec(memory_space=pltpu.VMEM)
     smem = pl.BlockSpec(memory_space=pltpu.SMEM)
-    sent, own, aside = pl.pallas_call(
+    sent, own, left, aside = pl.pallas_call(
         pack_kernel,
         out_shape=(
-            pltpu.VMEM((ROWS, width), jnp.bfloat16),
+            pltpu.VMEM((ROWS, HEAD), jnp.bfloat16),
             pltpu.VMEM((ROWS, width), jnp.float32),
+            pltpu.VMEM((2 * ROWS, HEAD), jnp.bfloat16),
             pltpu.VMEM((ROWS, 128), jnp.float32),
         ),
         in_specs=[vmem, vmem, vmem, smem],
-        out_specs=(vmem, vmem, vmem),
+        out_specs=(vmem, vmem, vmem, vmem),
     )(images, captions, caption_owner, caption_count)
-    mine = gather(sent)
+    near, scalars = pl.pallas_call(
+        scalars_kernel,
+        out_shape=(pltpu.VMEM((ROWS, HEAD), jnp.bfloat16), pltpu.VMEM((ROWS, 128), jnp.float32)),
+        in_specs=[smem, smem, vmem],
+        out_specs=(vmem, vmem),
+    )(log_scale, bias, sent)
+    mine = gather(sent, near)
     other = lax.ppermute(mine, "core", [(0, 1), (1, 0)])
+    limits = pltpu.CompilerParams(vmem_limit_bytes=32 * 1024 * 1024)
+    kernel = functools.partial(pair_kernel, chips, packers, pair_rows, slots)
+    loss, upstream = pl.pallas_call(
+        functools.partial(kernel, False),
+        out_shape=(pltpu.VMEM((ROWS, 128), jnp.float32), pltpu.VMEM((2 * ROWS, HEAD), jnp.float32)),
+        in_specs=[vmem] * 4,
+        out_specs=(vmem, vmem),
+        compiler_params=limits,
+        cost_estimate=pl.CostEstimate(flops=64 * HEAD * mine.shape[0], bytes_accessed=2 * mine.size, transcendentals=0),
+    )(left, aside, scalars, mine)
     row_loss, grad_images, grad_captions = pl.pallas_call(
-        functools.partial(pair_kernel, chips, packers, pair_rows, slots),
+        functools.partial(kernel, True),
         out_shape=(
             jax.ShapeDtypeStruct((1, pair_rows), jnp.float32),
             jax.ShapeDtypeStruct(images.shape, jnp.float32),
             jax.ShapeDtypeStruct(captions.shape, jnp.float32),
         ),
-        in_specs=[smem] * 2 + [vmem] * 4,
+        in_specs=[vmem] * 7,
         out_specs=(vmem, vmem, vmem),
-        compiler_params=pltpu.CompilerParams(vmem_limit_bytes=32 * 1024 * 1024),
-    )(log_scale, bias, own, aside, mine, other)
+        compiler_params=limits,
+    )(left, aside, scalars, other, own, loss, upstream)
     return row_loss.reshape(pair_rows), grad_images, grad_captions
 
 

time: 21.2 us -> 20.8 us (0.981)
  waiting for transfers between devices: 7.09 us -> 5.38 us
  Pallas kernels: 2.11 us -> 3.27 us
    ppermute x6, waiting for transfers between devices: 6.9 us -> 4.45 us  [gather(): taken.append(lax.ppermute(rows, ('chip', 'core', 'pack'), pairs))]
    pallas_call x2 -> x4, Pallas kernels: 2.11 us -> 3.27 us  [the longest x1 1.19 us: body(): pl.pallas_call(functools.partial(kernel, True), out_shape=(jax.ShapeDtype...]
    ppermute x1, waiting for transfers between devices: 0.2 us -> 0.92 us  [body(): other = lax.ppermute(mine, 'core', [(0, 1), (1, 0)])]
  transfers between devices with their start and end apart: 7 -> 7, of which waited for: 4 -> 4; matrix products, arithmetic and copies ran while one was open for 0% -> 0% of each run, Pallas kernels for 0% -> 6%
where the time goes in v3:
time: 20.8 us; the launch traced here: 20.5 us
  starting transfers between devices  9.15 us (44%)
  waiting for transfers between devices  5.38 us (26%)
  Pallas kernels  3.27 us (16%)
  between operations  2.61 us (13%)
    ppermute x6, starting transfers between devices, gather(): taken.append(lax.ppermute(rows, ('chip', 'core', 'pack'), pairs))  9 us
    ppermute x6, waiting for transfers between devices, gather(): taken.append(lax.ppermute(rows, ('chip', 'core', 'pack'), pairs))  4.45 us
    pallas_call x1, Pallas kernels, body(): pl.pallas_call(functools.partial(kernel, True), out_shape=(jax.ShapeDtype...  1.19 us
    ppermute x1, waiting for transfers between devices, body(): other = lax.ppermute(mine, 'core', [(0, 1), (1, 0)])  0.92 us
    pallas_call x1, Pallas kernels, body(): pl.pallas_call(pack_kernel, out_shape=(pltpu.VMEM((ROWS, HEAD), jnp.bfloa...  0.88 us
    pallas_call x1, Pallas kernels, body(): pl.pallas_call(scalars_kernel, out_shape=(pltpu.VMEM((ROWS, HEAD), jnp.bf...  0.72 us
    pallas_call x1, Pallas kernels, body(): pl.pallas_call(functools.partial(kernel, False), out_shape=(pltpu.VMEM((R...  0.48 us
  transfers between devices with their start and end apart: 7, of which 4 were waited for; matrix products, arithmetic and copies ran while one was open for 0% of the time, Pallas kernels for 6%

profile of v3, /device:TPU:0, one launch (start us, length us, event | category | flops | bytes accessed | tf_op | source)
XLA Modules:
  0.0 20.5 jit_solution(3912122587645411490)
XLA Ops:
  1.3 0.9 %shard_map.85 = (bf16[8,896]{1,0:T(8,128)(2,1)S(1)}, f32[8,1152]{1,0:T(8,128)S(1)}, bf16[16,896]{1,0:T(8,128)(2,1)S(1)}, f32[8,128]{1,0:T(8,128)S(1)}) custom-call(bf16[2,1152]{1,0:T(2,128)(2,1)} %images_ref.1, bf16[4,1152]{1,0:T(4,128)(2,1)} %captions_ref.1, s32[4]{0:T(128)} %owner_ref.1, s32[1]{0:T(128)S(6)} %copy.18.count_ref), custom_call_target="tpu_custom_call" | custom-call | tf_op jit(solution)/shard_map/pallas_call | solution.py:227
  2.2 0.0 copy-start
  2.2 3.5 %collective-permute-start = (bf16[8,896]{1,0:T(8,128)(2,1)S(1)}, bf16[8,896]{1,0:T(8,128)(2,1)S(1)}, u32[]{:S(2)}, u32[]{:S(2)}) collective-permute-start(bf16[8,896]{1,0:T(8,128)(2,1)S(1)} %get-tuple-element.16.sent_ref), channel_id=1, source_target_pairs={{0,20},{1,21},{2,22},{3,23},{4,16},{5,17},{6,18},{7,19},{8,28},{9,... | collective-permute-start | bytes 43016 | tf_op jit(solution)/shard_map/ppermute | solution.py:200
  5.7 1.6 %collective-permute-start.1 = (bf16[8,896]{1,0:T(8,128)(2,1)S(1)}, bf16[8,896]{1,0:T(8,128)(2,1)S(1)}, u32[]{:S(2)}, u32[]{:S(2)}) collective-permute-start(bf16[8,896]{1,0:T(8,128)(2,1)S(1)} %get-tuple-element.16.sent_ref), channel_id=1, source_target_pairs={{0,28},{1,29},{2,30},{3,31},{4,24},{5,25},{6,26},{7,27},{8,20},{9,... | collective-permute-start | bytes 43016 | tf_op jit(solution)/shard_map/ppermute | solution.py:200
  7.3 0.2 %collective-permute-start.2 = (bf16[8,896]{1,0:T(8,128)(2,1)S(1)}, bf16[8,896]{1,0:T(8,128)(2,1)S(1)}, u32[]{:S(2)}, u32[]{:S(2)}) collective-permute-start(bf16[8,896]{1,0:T(8,128)(2,1)S(1)} %get-tuple-element.16.sent_ref), channel_id=1, source_target_pairs={{0,12},{1,13},{2,14},{3,15},{4,8},{5,9},{6,10},{7,11},{8,4},{9,5},... | collective-permute-start | bytes 43016 | tf_op jit(solution)/shard_map/ppermute | solution.py:200
  8.9 0.0 copy-done
  8.9 0.7 %shard_map.86 = (bf16[8,896]{1,0:T(8,128)(2,1)S(1)}, f32[8,128]{1,0:T(8,128)S(1)}) custom-call(f32[1]{0:T(128)S(6)} %copy.19.scale_ref, f32[1]{0:T(128)S(6)} %copy.20.bias_ref, bf16[8,896]{1,0:T(8,128)(2,1)} %copy-done), custom_call_target="tpu_custom_call" | custom-call | tf_op jit(solution)/shard_map/pallas_call | solution.py:238
  9.6 0.0 collective-permute-done
  9.6 1.0 %collective-permute-done.1 = bf16[8,896]{1,0:T(8,128)(2,1)S(1)} collective-permute-done((bf16[8,896]{1,0:T(8,128)(2,1)S(1)}, bf16[8,896]{1,0:T(8,128)(2,1)S(1)}, u32[]{:S(2)}, u32[]{:S(2)}) %collective-permute-start.1) | collective-permute-done | bytes 14368 | tf_op jit(solution)/shard_map/ppermute | solution.py:200
  10.7 0.0 collective-permute-done.2
  10.7 2.8 %collective-permute-start.3 = (bf16[32,896]{1,0:T(8,128)(2,1)S(1)}, bf16[32,896]{1,0:T(8,128)(2,1)S(1)}, u32[]{:S(2)}, u32[]{:S(2)}) collective-permute-start(bf16[32,896]{1,0:T(8,128)(2,1)S(1)} %get-tuple-element.25), channel_id=1, source_target_pairs={{0,7},{1,6},{2,5},{3,4},{4,3},{5,2},{6,1},{7,0},{8,15},{9,14},{10,... | collective-permute-start | bytes 172040 | tf_op jit(solution)/shard_map/ppermute | solution.py:200
  13.5 0.0 collective-permute-start.4
  13.5 0.8 %collective-permute-start.5 = (bf16[32,896]{1,0:T(8,128)(2,1)S(1)}, bf16[32,896]{1,0:T(8,128)(2,1)S(1)}, u32[]{:S(2)}, u32[]{:S(2)}) collective-permute-start(bf16[32,896]{1,0:T(8,128)(2,1)S(1)} %get-tuple-element.25), channel_id=1, source_target_pairs={{0,5},{1,4},{2,7},{3,6},{4,1},{5,0},{6,3},{7,2},{8,13},{9,12},{10,... | collective-permute-start | bytes 172040 | tf_op jit(solution)/shard_map/ppermute | solution.py:200
  14.3 1.5 %collective-permute-done.3 = bf16[32,896]{1,0:T(8,128)(2,1)S(1)} collective-permute-done((bf16[32,896]{1,0:T(8,128)(2,1)S(1)}, bf16[32,896]{1,0:T(8,128)(2,1)S(1)}, u32[]{:S(2)}, u32[]{:S(2)}) %collective-permute-start.3) | collective-permute-done | bytes 57376 | tf_op jit(solution)/shard_map/ppermute | solution.py:200
  15.8 1.9 %collective-permute-done.4 = bf16[32,896]{1,0:T(8,128)(2,1)S(1)} collective-permute-done((bf16[32,896]{1,0:T(8,128)(2,1)S(1)}, bf16[32,896]{1,0:T(8,128)(2,1)S(1)}, u32[]{:S(2)}, u32[]{:S(2)}) %collective-permute-start.4) | collective-permute-done | bytes 57376 | tf_op jit(solution)/shard_map/ppermute | solution.py:200
  17.7 0.0 collective-permute-done.5
  17.7 0.2 collective-permute-start.6
  17.9 0.5 %shard_map.87 = (f32[8,128]{1,0:T(8,128)S(1)}, f32[16,896]{1,0:T(8,128)S(1)}) custom-call(bf16[16,896]{1,0:T(8,128)(2,1)S(1)} %get-tuple-element.14.refs_0_, f32[8,128]{1,0:T(8,128)S(1)} %get-tuple-element.15.refs_1_, f32[8,128]{1,0:T(8,128)S(1)} %get-tuple-element.17.refs_2_, bf16[128,896]{1,0:T(8,128)(2,1)S(1)} %constant_dynamic-update-slice_fusion.4.refs_3_), custom_call_target="tpu_custom_call" | custom-call | flops 7340032 | bytes 229376 | tf_op jit(solution)/shard_map/pallas_call | solution.py:248
  18.4 0.9 %collective-permute-done.6.refs_3_ = bf16[128,896]{1,0:T(8,128)(2,1)S(1)} collective-permute-done((bf16[128,896]{1,0:T(8,128)(2,1)S(1)}, bf16[128,896]{1,0:T(8,128)(2,1)S(1)}, u32[]{:S(2)}, u32[]{:S(2)}) %collective-permute-start.6) | collective-permute-done | bytes 229408 | tf_op jit(solution)/shard_map/ppermute | solution.py:245
  19.3 1.2 %shard_map.88 = (f32[1,2]{1,0:T(1,128)}, f32[2,1152]{1,0:T(2,128)}, f32[4,1152]{1,0:T(4,128)}) custom-call(bf16[16,896]{1,0:T(8,128)(2,1)S(1)} %get-tuple-element.14.refs_0_, f32[8,128]{1,0:T(8,128)S(1)} %get-tuple-element.15.refs_1_, f32[8,128]{1,0:T(8,128)S(1)} %get-tuple-element.17.refs_2_, bf16[128,896]{1,0:T(8,128)(2,1)S(1)} %collective-permute-done.6.refs_3_, ...), custom_call_target="tpu_custom_call" | custom-call | tf_op jit(solution)/shard_map/pallas_call | solution.py:256
  (7 shorter events, 0.1 us)
Async XLA Ops:
  2.2 6.7 %copy-start = (bf16[8,896]{1,0:T(8,128)(2,1)}, bf16[8,896]{1,0:T(8,128)(2,1)S(1)}, u32[]{:S(2)}) copy-start(bf16[8,896]{1,0:T(8,128)(2,1)S(1)} %get-tuple-element.16.sent_ref) | copy-start | bytes 43012
  2.2 7.4 %collective-permute-start = (bf16[8,896]{1,0:T(8,128)(2,1)S(1)}, bf16[8,896]{1,0:T(8,128)(2,1)S(1)}, u32[]{:S(2)}, u32[]{:S(2)}) collective-permute-start(bf16[8,896]{1,0:T(8,128)(2,1)S(1)} %get-tuple-element.16.sent_ref), channel_id=1, source_target_pairs={{0,20},{1,21},{2,22},{3,23},{4,16},{5,17},{6,18},{7,19},{8,28},{9,... | collective-permute-start | bytes 43016 | tf_op jit(solution)/shard_map/ppermute | solution.py:200
  5.7 4.9 %collective-permute-start.1 = (bf16[8,896]{1,0:T(8,128)(2,1)S(1)}, bf16[8,896]{1,0:T(8,128)(2,1)S(1)}, u32[]{:S(2)}, u32[]{:S(2)}) collective-permute-start(bf16[8,896]{1,0:T(8,128)(2,1)S(1)} %get-tuple-element.16.sent_ref), channel_id=1, source_target_pairs={{0,28},{1,29},{2,30},{3,31},{4,24},{5,25},{6,26},{7,27},{8,20},{9,... | collective-permute-start | bytes 43016 | tf_op jit(solution)/shard_map/ppermute | solution.py:200
  7.3 3.3 %collective-permute-start.2 = (bf16[8,896]{1,0:T(8,128)(2,1)S(1)}, bf16[8,896]{1,0:T(8,128)(2,1)S(1)}, u32[]{:S(2)}, u32[]{:S(2)}) collective-permute-start(bf16[8,896]{1,0:T(8,128)(2,1)S(1)} %get-tuple-element.16.sent_ref), channel_id=1, source_target_pairs={{0,12},{1,13},{2,14},{3,15},{4,8},{5,9},{6,10},{7,11},{8,4},{9,5},... | collective-permute-start | bytes 43016 | tf_op jit(solution)/shard_map/ppermute | solution.py:200
  10.7 5.1 %collective-permute-start.3 = (bf16[32,896]{1,0:T(8,128)(2,1)S(1)}, bf16[32,896]{1,0:T(8,128)(2,1)S(1)}, u32[]{:S(2)}, u32[]{:S(2)}) collective-permute-start(bf16[32,896]{1,0:T(8,128)(2,1)S(1)} %get-tuple-element.25), channel_id=1, source_target_pairs={{0,7},{1,6},{2,5},{3,4},{4,3},{5,2},{6,1},{7,0},{8,15},{9,14},{10,... | collective-permute-start | bytes 172040 | tf_op jit(solution)/shard_map/ppermute | solution.py:200
  13.5 4.2 %collective-permute-start.4 = (bf16[32,896]{1,0:T(8,128)(2,1)S(1)}, bf16[32,896]{1,0:T(8,128)(2,1)S(1)}, u32[]{:S(2)}, u32[]{:S(2)}) collective-permute-start(bf16[32,896]{1,0:T(8,128)(2,1)S(1)} %get-tuple-element.25), channel_id=1, source_target_pairs={{0,6},{1,7},{2,4},{3,5},{4,2},{5,3},{6,0},{7,1},{8,14},{9,15},{10,... | collective-permute-start | bytes 172040 | tf_op jit(solution)/shard_map/ppermute | solution.py:200
  13.5 4.2 %collective-permute-start.5 = (bf16[32,896]{1,0:T(8,128)(2,1)S(1)}, bf16[32,896]{1,0:T(8,128)(2,1)S(1)}, u32[]{:S(2)}, u32[]{:S(2)}) collective-permute-start(bf16[32,896]{1,0:T(8,128)(2,1)S(1)} %get-tuple-element.25), channel_id=1, source_target_pairs={{0,5},{1,4},{2,7},{3,6},{4,1},{5,0},{6,3},{7,2},{8,13},{9,12},{10,... | collective-permute-start | bytes 172040 | tf_op jit(solution)/shard_map/ppermute | solution.py:200
  17.7 1.6 %collective-permute-start.6 = (bf16[128,896]{1,0:T(8,128)(2,1)S(1)}, bf16[128,896]{1,0:T(8,128)(2,1)S(1)}, u32[]{:S(2)}, u32[]{:S(2)}) collective-permute-start(bf16[128,896]{1,0:T(8,128)(2,1)S(1)} %constant_dynamic-update-slice_fusion.4.refs_3_), channel_id=1, source_target_pairs={{0,4},{4,0},{1,5},{5,1},{2,6},{6,2},{3,7},{7,3},{8,12},{12,8},{9,1... | collective-permute-start | bytes 688136 | tf_op jit(solution)/shard_map/ppermute | solution.py:245
